TPU v7x, 32 devices: a whole 2x2x4 slice. The times are simulated.
32 devices in a mesh: req: 8 (over y, x, core), tp: 4 (over z).
Axes of the slice: x: 2, y: 2, z: 4, core: 2. Of those that a mesh axis runs over, the one named last changes fastest.
Arguments:
- hidden_in: bfloat16 [8192, 2048], P('req'), may hold values from -6 to 6
- norm_gain: bfloat16 [2048], replicated, may hold values from 0.099609375 to 1.8984375
- w_query: bfloat16 [2048, 1280], P(None, 'tp'), may hold values from -0.125 to 0.125
- key_value_weight: bfloat16 [2048, 640], replicated, may hold values from -0.3125 to 0.3125
- w_out: bfloat16 [1280, 2048], replicated, may hold values from -0.625 to 0.625
- prior_cache: bfloat16 [8, 7168, 640], P('req'), may hold values from -52 to 52
- cache_len: int32 [8], P('req'), may hold values from 1 to 7168, 28672 in all
- group_len: int32 [8], P('req'), may hold values from 1 to 1024, 4096 in all
- page_map: int32 [8, 32], P('req'), may hold values from 0 to 31, each once within a row
Outputs:
- hidden_out: bfloat16 [8192, 2048], P(('req', 'tp'))
- decode_kv: bfloat16 [32, 8, 256, 640], P(('req', 'tp'))
Inputs may be any that keep to these rules, and one draw needn't show every extreme that they name: `page_map`: each row names every device index once.
All inputs are finite; a program needn't handle non-finite values. No bound on the sum of `cache_len` or of `group_len` on one device may be relied on, other than what follows from the above.
Results may differ from a plain program's by a relative error of at most 0.014.
The roundings to bfloat16 on the way count: a program that leaves them out, or rounds other values in their place, can miss the bound.
Values may be sent and summed in bfloat16 or wider, within the bound.
A program may use at most 128 MiB of HBM per device.

v0:
```python
import functools
import math

import jax
import jax.numpy as jnp
from jax import lax
from jax.experimental import pallas as pl
from jax.experimental.pallas import tpu as pltpu
from jax.sharding import PartitionSpec as P

QUERY_HEAD_COUNT = 20
KEY_VALUE_HEADS = 5
HEAD_SIZE = 64
NEW_TOKEN_SLOTS = 1024
PRIOR_SLOTS = 7168
KEY_WIDTH = KEY_VALUE_HEADS * HEAD_SIZE
KEYS = 512
TILE = 256
PAIR = 2 * HEAD_SIZE
VALUE_ROWS = 80
LANES = 128
QUERY_SCALE = HEAD_SIZE ** (-0.5) * math.log2(math.e)
VMEM_BYTES = 50 * 1024 * 1024


def project_kernel(
    hidden_ref, gain_ref, query_weight_ref, keyval_weight_ref, cosine_ref, sine_ref, q_ref, kv_ref
):
    half = HEAD_SIZE // 2
    hidden = hidden_ref[...].astype(jnp.float32)
    normed = (
        hidden
        * lax.rsqrt(jnp.mean(hidden * hidden, axis=-1, keepdims=True) + 1e-05)
        * gain_ref[...].astype(jnp.float32)
    ).astype(jnp.bfloat16)
    cosine, sine = cosine_ref[...], sine_ref[...]

    turned = lax.dot_general(
        query_weight_ref[...], normed, (((1,), (1,)), ((), ())), preferred_element_type=jnp.float32
    )
    for head in range(q_ref.shape[0]):
        first = turned[head * HEAD_SIZE : head * HEAD_SIZE + half]
        second = turned[head * HEAD_SIZE + half : (head + 1) * HEAD_SIZE]
        q_ref[head, :half] = ((first * cosine - second * sine) * QUERY_SCALE).astype(jnp.bfloat16)
        q_ref[head, half:] = ((second * cosine + first * sine) * QUERY_SCALE).astype(jnp.bfloat16)

    keyval = jnp.dot(normed, keyval_weight_ref[...], preferred_element_type=jnp.float32)
    covered = (KEY_WIDTH + LANES - 1) // LANES * LANES
    repeat = LANES // half
    lanes_cosine = jnp.concatenate([jnp.concatenate([cosine] * repeat, axis=0).T] * (covered // LANES), axis=1)
    lanes_sine = jnp.concatenate([jnp.concatenate([sine] * repeat, axis=0).T] * (covered // LANES), axis=1)
    start = keyval[:, :covered]
    lane = lax.broadcasted_iota(jnp.int32, start.shape, 1)
    swapped = jnp.where(
        lane % HEAD_SIZE < half,
        -pltpu.roll(start, covered - half, 1),
        pltpu.roll(start, half, 1),
    )
    rotated = start * lanes_cosine + swapped * lanes_sine
    kv_ref[:, :covered] = jnp.where(lane < KEY_WIDTH, rotated, start).astype(jnp.bfloat16)
    kv_ref[:, covered:] = keyval[:, covered:].astype(jnp.bfloat16)


def project(hidden, gain, query_weight, keyval_weight, cosine, sine):
    rows, width = hidden.shape
    heads = query_weight.shape[0] // HEAD_SIZE
    half = HEAD_SIZE // 2
    return pl.pallas_call(
        project_kernel,
        grid=(rows // TILE,),
        in_specs=[
            pl.BlockSpec((TILE, width), lambda i: (i, 0)),
            pl.BlockSpec((1, width), lambda i: (0, 0)),
            pl.BlockSpec(query_weight.shape, lambda i: (0, 0)),
            pl.BlockSpec(keyval_weight.shape, lambda i: (0, 0)),
            pl.BlockSpec((half, TILE), lambda i: (0, i)),
            pl.BlockSpec((half, TILE), lambda i: (0, i)),
        ],
        out_specs=[
            pl.BlockSpec((heads, HEAD_SIZE, TILE), lambda i: (0, 0, i)),
            pl.BlockSpec((TILE, 2 * KEY_WIDTH), lambda i: (i, 0)),
        ],
        out_shape=[
            jax.ShapeDtypeStruct((heads, HEAD_SIZE, rows), jnp.bfloat16),
            jax.ShapeDtypeStruct((rows, 2 * KEY_WIDTH), jnp.bfloat16),
        ],
        compiler_params=pltpu.CompilerParams(vmem_limit_bytes=VMEM_BYTES),
    )(hidden, gain, query_weight, keyval_weight, cosine, sine)


def ship_kernel(block_rows, count, picks, sizes, prior_ref, fresh_ref, out_ref, sems):
    prior_blocks = PRIOR_SLOTS // block_rows

    def rows_of(block):
        return pl.ds(pl.multiple_of(block * block_rows, block_rows), block_rows)

    @pl.loop(0, count)
    def _(i):
        pick = picks[i]

        @pl.when(pick < prior_blocks)
        def _():
            pltpu.make_async_copy(prior_ref.at[rows_of(pick)], out_ref.at[i], sems.at[i]).start()

        @pl.when(pick >= prior_blocks)
        def _():
            pltpu.make_async_copy(
                fresh_ref.at[rows_of(pick - prior_blocks)], out_ref.at[i], sems.at[i]
            ).start()

    @pl.loop(0, count)
    def _(i):
        pick = picks[i]
        is_prior = pick < prior_blocks
        base = jnp.where(is_prior, pick, pick - prior_blocks) * block_rows
        live = jnp.where(is_prior, sizes[0], sizes[1])
        pltpu.make_async_copy(prior_ref.at[rows_of(0)], out_ref.at[i], sems.at[i]).wait()

        @pl.when(base + block_rows > live)
        def _():
            row = base + lax.broadcasted_iota(jnp.int32, (block_rows, 1), 0)
            out_ref[i] = jnp.where(row < live, out_ref[i], jnp.zeros((), jnp.bfloat16))


def pick_blocks(picks, sizes, prior, fresh, block_rows):
    count, width = picks.shape[0], prior.shape[1]
    return pl.pallas_call(
        functools.partial(ship_kernel, block_rows, count),
        in_specs=[
            pl.BlockSpec(memory_space=pltpu.SMEM),
            pl.BlockSpec(memory_space=pltpu.SMEM),
            pl.BlockSpec(memory_space=pl.ANY),
            pl.BlockSpec(memory_space=pl.ANY),
        ],
        out_specs=pl.BlockSpec(memory_space=pltpu.VMEM),
        out_shape=jax.ShapeDtypeStruct((count, block_rows, width), jnp.bfloat16),
        scratch_shapes=[pltpu.SemaphoreType.DMA((count,))],
        compiler_params=pltpu.CompilerParams(vmem_limit_bytes=VMEM_BYTES),
    )(picks, sizes, prior, fresh)


def attention_kernel(
    heads, sizes, q_ref, prior_ref, fresh_ref, out_ref, staged, keys, values, q_pair, top, acc, sems
):
    cached, fresh, first_kv = sizes[0], sizes[1], sizes[2]
    split = sizes[3]
    tiles = (fresh + TILE - 1) // TILE
    prior_live = (cached + KEYS - 1) // KEYS
    prior_whole = cached // KEYS
    remainder = cached - prior_whole * KEYS

    def fetch(block):
        rows = pl.ds(pl.multiple_of(block * KEYS, KEYS), KEYS)
        return pltpu.make_async_copy(prior_ref.at[rows], staged.at[rows], sems.at[block])

    @pl.loop(0, prior_live)
    def _(block):
        fetch(block).start()

    key_start = first_kv * HEAD_SIZE
    row_in = lax.broadcasted_iota(jnp.int32, (2 * KEY_WIDTH, PAIR), 0)
    lane_in = lax.broadcasted_iota(jnp.int32, (2 * KEY_WIDTH, PAIR), 1)
    choose_keys = (row_in == lane_in + key_start).astype(jnp.float32).astype(jnp.bfloat16)
    row_out = lax.broadcasted_iota(jnp.int32, (PAIR, 2 * KEY_WIDTH), 0)
    lane_out = lax.broadcasted_iota(jnp.int32, (PAIR, 2 * KEY_WIDTH), 1)
    choose_values = (
        (lane_out == row_out + key_start + KEY_WIDTH).astype(jnp.float32).astype(jnp.bfloat16)
    )

    def unpack(rows, at, count):
        keys[pl.ds(at, count), :] = jnp.dot(
            rows, choose_keys, preferred_element_type=jnp.float32
        ).astype(jnp.bfloat16)
        turned = lax.dot_general(
            choose_values, rows, (((1,), (1,)), ((), ())), preferred_element_type=jnp.float32
        ).astype(jnp.bfloat16)
        ones = jnp.ones((VALUE_ROWS - HEAD_SIZE, count), jnp.bfloat16)
        for half in range(2):
            values[half, :HEAD_SIZE, pl.ds(at, count)] = turned[
                half * HEAD_SIZE : (half + 1) * HEAD_SIZE
            ]
            values[half, HEAD_SIZE:, pl.ds(at, count)] = ones

    @pl.loop(0, tiles)
    def _(tile):
        rows = pl.ds(pl.multiple_of(tile * TILE, TILE), TILE)
        unpack(fresh_ref[rows, :], pl.multiple_of(PRIOR_SLOTS + tile * TILE, TILE), TILE)

    @pl.loop(0, prior_live)
    def _(block):
        fetch(block).wait()
        at = pl.multiple_of(block * KEYS, KEYS)
        unpack(staged[pl.ds(at, KEYS), :], at, KEYS)

    out_ref[...] = jnp.zeros_like(out_ref)

    def step(starts, count, allowed):
        items = [(at, head) for at in starts for head in range(heads)]

        def score(at, head):
            return jnp.dot(
                keys[pl.ds(at, count), :], q_pair[head], preferred_element_type=jnp.float32
            )

        def gather_values(at, head, rescale, chances):
            group = jnp.where(head < split, 0, 1)
            acc[head] = acc[head] * rescale + jnp.dot(
                values[group, :, pl.ds(at, count)], chances, preferred_element_type=jnp.float32
            )

        ahead = score(*items[0])
        pending = None
        for index, (at, head) in enumerate(items):
            scores = ahead
            if index + 1 < len(items):
                ahead = score(*items[index + 1])
            if allowed is not None:
                scores = jnp.where(allowed, scores, -1e30)
            old = top[head]
            new = jnp.maximum(old, jnp.max(scores, axis=0, keepdims=True))
            top[head] = new
            chances = jnp.exp2((scores - new).astype(jnp.bfloat16))
            if pending is not None:
                gather_values(*pending)
            pending = (at, head, jnp.exp2(old - new), chances)
        gather_values(*pending)

    @pl.loop(0, tiles)
    def _(tile):
        columns = pl.ds(pl.multiple_of(tile * TILE, TILE), TILE)
        for head in range(heads):
            query = q_ref[head, :, columns]
            none = jnp.zeros_like(query)
            lower = head < split
            q_pair[head, :HEAD_SIZE] = jnp.where(lower, query, none)
            q_pair[head, HEAD_SIZE:] = jnp.where(lower, none, query)
        top[...] = jnp.full_like(top, -1e30)
        acc[...] = jnp.zeros_like(acc)

        @pl.loop(0, prior_whole // 2)
        def _(pair):
            at = pl.multiple_of(pair * (2 * KEYS), 2 * KEYS)
            step([at, pl.multiple_of(at + KEYS, KEYS)], KEYS, None)

        @pl.when(prior_whole % 2 == 1)
        def _():
            step([pl.multiple_of((prior_whole - 1) * KEYS, KEYS)], KEYS, None)

        @pl.when(remainder > 0)
        def _():
            index = lax.broadcasted_iota(jnp.int32, (KEYS, TILE), 0)
            step([pl.multiple_of(prior_whole * KEYS, KEYS)], KEYS, index < remainder)

        @pl.loop(0, tile)
        def _(block):
            step([pl.multiple_of(PRIOR_SLOTS + block * TILE, TILE)], TILE, None)

        index = lax.broadcasted_iota(jnp.int32, (TILE, TILE), 0)
        slot = lax.broadcasted_iota(jnp.int32, (TILE, TILE), 1)
        step([pl.multiple_of(PRIOR_SLOTS + tile * TILE, TILE)], TILE, index <= slot)
        for head in range(heads):
            total = acc[head]
            out_ref[tile, head * HEAD_SIZE : (head + 1) * HEAD_SIZE, :] = (
                total[:HEAD_SIZE] / total[HEAD_SIZE : HEAD_SIZE + 1]
            ).astype(jnp.bfloat16)


def attention(sizes, queries, prior, fresh_rows):
    heads = queries.shape[0]
    tiles = NEW_TOKEN_SLOTS // TILE
    context = PRIOR_SLOTS + NEW_TOKEN_SLOTS
    return pl.pallas_call(
        functools.partial(attention_kernel, heads),
        in_specs=[
            pl.BlockSpec(memory_space=pltpu.SMEM),
            pl.BlockSpec(memory_space=pltpu.VMEM),
            pl.BlockSpec(memory_space=pl.ANY),
            pl.BlockSpec(memory_space=pltpu.VMEM),
        ],
        out_specs=pl.BlockSpec(memory_space=pltpu.VMEM),
        out_shape=jax.ShapeDtypeStruct((tiles, heads * HEAD_SIZE, TILE), jnp.bfloat16),
        scratch_shapes=[
            pltpu.VMEM((PRIOR_SLOTS, 2 * KEY_WIDTH), jnp.bfloat16),
            pltpu.VMEM((context, PAIR), jnp.bfloat16),
            pltpu.VMEM((2, VALUE_ROWS, context), jnp.bfloat16),
            pltpu.VMEM((heads, PAIR, TILE), jnp.bfloat16),
            pltpu.VMEM((heads, 1, TILE), jnp.float32),
            pltpu.VMEM((heads, VALUE_ROWS, TILE), jnp.float32),
            pltpu.SemaphoreType.DMA((PRIOR_SLOTS // KEYS,)),
        ],
        compiler_params=pltpu.CompilerParams(vmem_limit_bytes=VMEM_BYTES),
        cost_estimate=pl.CostEstimate(
            flops=4 * NEW_TOKEN_SLOTS * heads * context * PAIR,
            bytes_accessed=2 * context * 2 * KEY_WIDTH,
            transcendentals=NEW_TOKEN_SLOTS * heads * context,
        ),
    )(sizes, queries, prior, fresh_rows)


def after_kernel(value_ref, other_ref, out_ref):
    del value_ref, other_ref, out_ref


def after(value, other):
    return pl.pallas_call(
        after_kernel,
        in_specs=[pl.BlockSpec(memory_space=pl.ANY)] * 2,
        out_specs=pl.BlockSpec(memory_space=pl.ANY),
        out_shape=jax.ShapeDtypeStruct(value.shape, value.dtype),
        input_output_aliases={0: 0},
    )(value, other)


def shards(
    hidden_in,
    norm_gain,
    w_query,
    key_value_weight,
    w_out,
    prior_cache,
    cache_len,
    group_len,
    page_map,
):
    rank = lax.axis_index("tp")
    tp_count = lax.axis_size("tp")
    req_count = lax.axis_size("req")
    span = hidden_in.shape[0] // tp_count
    heads = w_query.shape[1] // HEAD_SIZE
    blocks = page_map.shape[1]
    block_rows = (PRIOR_SLOTS + NEW_TOKEN_SLOTS) // blocks
    cached, fresh = cache_len[0], group_len[0]

    positions = cached + jnp.arange(NEW_TOKEN_SLOTS, dtype=jnp.int32)
    half = HEAD_SIZE // 2
    frequency = 10000.0 ** (-(jnp.arange(half, dtype=jnp.float32) * 2.0 / HEAD_SIZE))
    angles = frequency[:, None] * positions.astype(jnp.float32)[None, :]
    queries, fresh_rows = project(
        hidden_in, norm_gain[None], w_query.T, key_value_weight, jnp.cos(angles), jnp.sin(angles)
    )

    targets = jnp.arange(req_count, dtype=jnp.int32) * tp_count + rank
    picks = jnp.sum(
        jnp.where(
            page_map[0][None, :] == targets[:, None],
            jnp.arange(blocks, dtype=jnp.int32)[None, :],
            0,
        ),
        axis=1,
    ).astype(jnp.int32)
    first_head = rank * heads
    group = QUERY_HEAD_COUNT // KEY_VALUE_HEADS
    first_kv = first_head // group
    split = (first_kv + 1) * group - first_head
    sizes = jnp.stack([cached, fresh, first_kv, split]).astype(jnp.int32)

    shipment = pick_blocks(picks, sizes, prior_cache[0], fresh_rows, block_rows)
    decode_kv = lax.all_to_all(shipment, "req", split_axis=0, concat_axis=0, tiled=True)[None]

    attended = attention(sizes, queries, prior_cache[0], fresh_rows)
    attended = after(attended, decode_kv)
    gathered = lax.all_to_all(attended, "tp", split_axis=0, concat_axis=0, tiled=True)
    mixed = lax.dot_general(
        gathered.reshape(QUERY_HEAD_COUNT * HEAD_SIZE, span),
        w_out,
        (((0,), (0,)), ((), ())),
        preferred_element_type=jnp.float32,
    )
    live = rank * span + jnp.arange(span, dtype=jnp.int32) < fresh
    own = lax.dynamic_slice_in_dim(hidden_in, rank * span, span, 0).astype(jnp.float32)
    hidden_out = jnp.where(live[:, None], own + mixed, 0.0).astype(jnp.bfloat16)
    return (hidden_out, decode_kv)


def solution(mesh):
    placed = (
        P("req", None),
        P(),
        P(None, "tp"),
        P(),
        P(),
        P("req", None, None),
        P("req"),
        P("req"),
        P("req", None),
    )
    return jax.shard_map(
        shards,
        mesh=mesh,
        in_specs=placed,
        out_specs=(P(("req", "tp"), None), P(("req", "tp"), None, None, None)),
        check_vma=False,
    )
```

profile of v0, /device:TPU:7, one launch (start us, length us, event | category | flops | bytes accessed | tf_op | source)
XLA Modules:
  0.0 103.6 jit_solution(1027577721514022632)
XLA Ops:
  2.0 0.7 broadcast_in_dim.36.gain_ref
  2.7 0.8 select_reduce_fusion.picks
  3.5 0.5 multiply_sine_fusion
  4.1 0.1 pad_add_fusion.sizes
  4.1 0.0 copy-start.1
  4.1 1.3 %copy-done.1 = bf16[2048,320]{0,1:T(8,128)(2,1)S(1)} copy-done((bf16[2048,320]{0,1:T(8,128)(2,1)S(1)}, bf16[2048,320]{0,1:T(8,128)(2,1)}, u32[]{:S(2)}) %copy-start.1) | copy-done | bytes 1310744
  5.5 8.8 %shard_map.104 = (bf16[5,64,1024]{2,1,0:T(8,128)(2,1)S(1)}, bf16[1024,640]{1,0:T(8,128)(2,1)S(1)}) custom-call(bf16[1024,2048]{1,0:T(8,128)(2,1)} %hidden_ref.1, bf16[1,2048]{1,0:T(2,128)(2,1)S(1)} %broadcast_in_dim.36.gain_ref, bf16[320,2048]{1,0:T(8,128)(2,1)S(1)} %bitcast.13, bf16[2048,640]{1,0:T(8,128)(2,1)} %keyval_weight_ref.1, ...), custom_call_target="tpu_custom_call" | custom-call | tf_op jit(solution)/shard_map/pallas_call | solution.py:68
  14.2 3.9 %shard_map.106 = bf16[8,256,640]{2,1,0:T(8,128)(2,1)} custom-call(s32[8]{0:T(128)S(1)} %select_reduce_fusion.picks, s32[4]{0:T(128)S(1)} %pad_add_fusion.sizes, bf16[7168,640]{1,0:T(8,128)(2,1)} %bitcast.14, bf16[1024,640]{1,0:T(8,128)(2,1)S(1)} %get-tuple-element.5.fresh_ref), custom_call_target="tpu_custom_call" | custom-call | tf_op jit(solution)/shard_map/pallas_call | solution.py:127
  18.1 4.5 %all-to-all-start = ((bf16[8,256,640]{2,1,0:T(8,128)(2,1)}), bf16[8,256,640]{2,1,0:T(8,128)(2,1)}, u32[]{:S(2)}, u32[]{:S(2)}) async-start(bf16[8,256,640]{2,1,0:T(8,128)(2,1)} %shard_map.106), calls=%async_computation | async-start | bytes 5242880 | tf_op jit(solution)/shard_map/all_to_all | solution.py:358
  22.6 55.7 %shard_map.105.value_ref = bf16[4,320,256]{2,1,0:T(8,128)(2,1)S(1)} custom-call(s32[4]{0:T(128)S(1)} %pad_add_fusion.sizes, bf16[5,64,1024]{2,1,0:T(8,128)(2,1)S(1)} %get-tuple-element.4.q_ref, bf16[7168,640]{1,0:T(8,128)(2,1)} %bitcast.15, bf16[1024,640]{1,0:T(8,128)(2,1)S(1)} %get-tuple-element.5.fresh_ref), custom_call_target="tpu_custom_call" | custom-call | flops 21474836480 | bytes 10485760 | tf_op jit(solution)/shard_map/pallas_call | solution.py:272
  78.2 0.0 copy-start
  78.3 0.8 copy-done
  79.1 0.0 all-to-all-done
  79.1 5.2 %all-to-all-start.1 = ((bf16[4,320,256]{2,1,0:T(8,128)(2,1)}), bf16[4,320,256]{2,1,0:T(8,128)(2,1)S(1)}, u32[]{:S(2)}, u32[]{:S(2)}) async-start(bf16[4,320,256]{2,1,0:T(8,128)(2,1)} %shard_map.107), calls=%async_computation.1 | async-start | bytes 1310720 | tf_op jit(solution)/shard_map/all_to_all | solution.py:362
  84.3 10.5 %all-to-all-done.1 = bf16[4,320,256]{2,1,0:T(8,128)(2,1)S(1)} async-done(((bf16[4,320,256]{2,1,0:T(8,128)(2,1)}), bf16[4,320,256]{2,1,0:T(8,128)(2,1)S(1)}, u32[]{:S(2)}, u32[]{:S(2)}) %all-to-all-start.1) | async-done | bytes 655392 | tf_op jit(solution)/shard_map/all_to_all | solution.py:362
  94.8 5.3 %fusion.1 = bf16[256,2048]{1,0:T(8,128)(2,1)} fusion(bf16[1280,256]{1,0:T(8,128)(2,1)S(1)} %bitcast.16, bf16[1280,2048]{1,0:T(8,128)(2,1)} %param.13, bf16[1024,2048]{1,0:T(8,128)(2,1)} %hidden_ref.1, s32[]{:T(128)S(6)} %select_n.16, pred[256]{0:T(512)(128)(4,1)S(1)} %add_compare_fusion), kind=kOutput, calls=%fused_computation.2 | convolution fusion | flops 1344274432 | bytes 7995652 | tf_op jit(solution)/shard_map/dot_general | solution.py:363
  100.1 3.5 %copy.16 = bf16[1,8,256,640]{3,2,1,0:T(8,128)(2,1)} copy(bf16[1,8,256,640]{3,2,1,0:T(8,128)(2,1)} %bitcast.7.other_ref) | data formatting | bytes 5242880
  (5 shorter events, 0.0 us)
Async XLA Ops:
  4.1 1.3 %copy-start.1 = (bf16[2048,320]{0,1:T(8,128)(2,1)S(1)}, bf16[2048,320]{0,1:T(8,128)(2,1)}, u32[]{:S(2)}) copy-start(bf16[2048,320]{0,1:T(8,128)(2,1)} %param.11) | copy-start | bytes 3932164
  18.1 61.0 %all-to-all-start = ((bf16[8,256,640]{2,1,0:T(8,128)(2,1)}), bf16[8,256,640]{2,1,0:T(8,128)(2,1)}, u32[]{:S(2)}, u32[]{:S(2)}) async-start(bf16[8,256,640]{2,1,0:T(8,128)(2,1)} %shard_map.106), calls=%async_computation | async-start | bytes 5242880 | tf_op jit(solution)/shard_map/all_to_all | solution.py:358
  78.2 0.8 copy-start
  79.1 15.7 %all-to-all-start.1 = ((bf16[4,320,256]{2,1,0:T(8,128)(2,1)}), bf16[4,320,256]{2,1,0:T(8,128)(2,1)S(1)}, u32[]{:S(2)}, u32[]{:S(2)}) async-start(bf16[4,320,256]{2,1,0:T(8,128)(2,1)} %shard_map.107), calls=%async_computation.1 | async-start | bytes 1310720 | tf_op jit(solution)/shard_map/all_to_all | solution.py:362
where the time goes:
time: 104 us
  Pallas kernels  68.3 us (66%)
  waiting for transfers between devices  10.5 us (10%)
  starting transfers between devices  9.62 us (9%)
  local copies, waits for them, and re-layouts  6.35 us (6%)
  matrix products  5.31 us (5%)
  between operations  2.01 us (2%)
  other arithmetic  1.48 us (1%)
    pallas_call x1, Pallas kernels, attention(): pl.pallas_call(functools.partial(attention_kernel, heads), in_specs=[pl.B...  55.7 us
    all_to_all x1, waiting for transfers between devices, shards(): lax.all_to_all(attended, 'tp', split_axis=0, concat_axis=0, tiled=True)  10.5 us
    pallas_call x1, Pallas kernels, project(): pl.pallas_call(project_kernel, grid=(rows // TILE,), in_specs=[pl.BlockSp...  8.78 us
    unnamed x5, local copies, waits for them, and re-layouts  5.65 us
    dot_general x1, matrix products, shards(): lax.dot_general(gathered.reshape(QUERY_HEAD_COUNT * HEAD_SIZE, span), w_o...  5.31 us
    all_to_all x1, starting transfers between devices, shards(): lax.all_to_all(attended, 'tp', split_axis=0, concat_axis=0, tiled=True)  5.17 us
    all_to_all x1, starting transfers between devices, shards(): lax.all_to_all(shipment, 'req', split_axis=0, concat_axis=0, tiled=True)  4.45 us
    pallas_call x1, Pallas kernels, pick_blocks(): pl.pallas_call(functools.partial(ship_kernel, block_rows, count), in_spec...  3.86 us
  transfers between devices with their start and end apart: 2, of which 1 were waited for; matrix products, arithmetic and copies ran while one was open for 0% of the time, Pallas kernels for 54%

commit v1 on v0

--- a/solution.py
+++ b/solution.py
@@ -237,9 +237,14 @@
         top[...] = jnp.full_like(top, -1e30)
         acc[...] = jnp.zeros_like(acc)
 
-        @pl.loop(0, prior_whole // 2)
-        def _(pair):
-            at = pl.multiple_of(pair * (2 * KEYS), 2 * KEYS)
+        @pl.loop(0, prior_whole // 4)
+        def _(quad):
+            at = pl.multiple_of(quad * (4 * KEYS), 4 * KEYS)
+            step([pl.multiple_of(at + part * KEYS, KEYS) for part in range(4)], KEYS, None)
+
+        @pl.when(prior_whole % 4 >= 2)
+        def _():
+            at = pl.multiple_of((prior_whole // 4) * (4 * KEYS), KEYS)
             step([at, pl.multiple_of(at + KEYS, KEYS)], KEYS, None)
 
         @pl.when(prior_whole % 2 == 1)
@@ -297,17 +302,24 @@
     )(sizes, queries, prior, fresh_rows)
 
 
-def after_kernel(value_ref, other_ref, out_ref):
-    del value_ref, other_ref, out_ref
+def after_kernel(value_ref, other_ref, out_ref, copied_ref, sem):
+    del value_ref, out_ref
+    copy = pltpu.make_async_copy(other_ref, copied_ref, sem)
+    copy.start()
+    copy.wait()
 
 
 def after(value, other):
     return pl.pallas_call(
         after_kernel,
         in_specs=[pl.BlockSpec(memory_space=pl.ANY)] * 2,
-        out_specs=pl.BlockSpec(memory_space=pl.ANY),
-        out_shape=jax.ShapeDtypeStruct(value.shape, value.dtype),
+        out_specs=[pl.BlockSpec(memory_space=pl.ANY)] * 2,
+        out_shape=[
+            jax.ShapeDtypeStruct(value.shape, value.dtype),
+            jax.ShapeDtypeStruct(other.shape, other.dtype),
+        ],
         input_output_aliases={0: 0},
+        scratch_shapes=[pltpu.SemaphoreType.DMA],
     )(value, other)
 
 
@@ -358,7 +370,7 @@
     decode_kv = lax.all_to_all(shipment, "req", split_axis=0, concat_axis=0, tiled=True)[None]
 
     attended = attention(sizes, queries, prior_cache[0], fresh_rows)
-    attended = after(attended, decode_kv)
+    attended, decode_kv = after(attended, decode_kv)
     gathered = lax.all_to_all(attended, "tp", split_axis=0, concat_axis=0, tiled=True)
     mixed = lax.dot_general(
         gathered.reshape(QUERY_HEAD_COUNT * HEAD_SIZE, span),

time: 104 us -> 194 us (1.87)
  Pallas kernels: 68.3 us -> 162 us
  local copies, waits for them, and re-layouts: 6.35 us -> 2.84 us
    pallas_call x1, Pallas kernels: 0.01 us -> 80.5 us  [after(): pl.pallas_call(after_kernel, in_specs=[pl.BlockSpec(memory_space=pl.ANY)]...]
    pallas_call x1, Pallas kernels: 55.7 us -> 69.1 us  [attention(): pl.pallas_call(functools.partial(attention_kernel, heads), in_specs=[pl.B...]
    unnamed x5 -> x4, local copies, waits for them, and re-layouts: 5.65 us -> 2.15 us
  transfers between devices with their start and end apart: 2 -> 2, of which waited for: 1 -> 1; matrix products, arithmetic and copies ran while one was open for 0% -> 0% of each run, Pallas kernels for 54% -> 36%
where the time goes in v1:
time: 194 us
  Pallas kernels  162 us (84%)
  waiting for transfers between devices  10.5 us (5%)
  starting transfers between devices  9.65 us (5%)
  matrix products  5.31 us (3%)
  local copies, waits for them, and re-layouts  2.84 us (1%)
  between operations  2.02 us (1%)
    pallas_call x1, Pallas kernels, after(): pl.pallas_call(after_kernel, in_specs=[pl.BlockSpec(memory_space=pl.ANY)]...  80.5 us
    pallas_call x1, Pallas kernels, attention(): pl.pallas_call(functools.partial(attention_kernel, heads), in_specs=[pl.B...  69.1 us
    all_to_all x1, waiting for transfers between devices, shards(): lax.all_to_all(attended, 'tp', split_axis=0, concat_axis=0, tiled=True)  10.5 us
    pallas_call x1, Pallas kernels, project(): pl.pallas_call(project_kernel, grid=(rows // TILE,), in_specs=[pl.BlockSp...  8.78 us
    dot_general x1, matrix products, shards(): lax.dot_general(gathered.reshape(QUERY_HEAD_COUNT * HEAD_SIZE, span), w_o...  5.31 us
    all_to_all x1, starting transfers between devices, shards(): lax.all_to_all(attended, 'tp', split_axis=0, concat_axis=0, tiled=True)  5.21 us
    all_to_all x1, starting transfers between devices, shards(): lax.all_to_all(shipment, 'req', split_axis=0, concat_axis=0, tiled=True)  4.43 us
  transfers between devices with their start and end apart: 2, of which 1 were waited for; matrix products, arithmetic and copies ran while one was open for 0% of the time, Pallas kernels for 36%

profile of v1, /device:TPU:7, one launch (start us, length us, event | category | flops | bytes accessed | tf_op | source)
XLA Modules:
  0.0 194.0 jit_solution(3368915038480069337)
XLA Ops:
  2.0 0.7 broadcast_in_dim.36.gain_ref
  2.7 0.8 select_reduce_fusion.picks
  3.5 0.5 multiply_sine_fusion
  4.1 0.1 pad_add_fusion.sizes
  4.1 0.0 copy-start.1
  4.1 1.3 copy-done.1
  5.5 8.8 %shard_map.104 = (bf16[5,64,1024]{2,1,0:T(8,128)(2,1)S(1)}, bf16[1024,640]{1,0:T(8,128)(2,1)S(1)}) custom-call(bf16[1024,2048]{1,0:T(8,128)(2,1)} %hidden_ref.1, bf16[1,2048]{1,0:T(2,128)(2,1)S(1)} %broadcast_in_dim.36.gain_ref, bf16[320,2048]{1,0:T(8,128)(2,1)S(1)} %bitcast.13, bf16[2048,640]{1,0:T(8,128)(2,1)} %keyval_weight_ref.1, ...), custom_call_target="tpu_custom_call" | custom-call | tf_op jit(solution)/shard_map/pallas_call | solution.py:68
  14.2 3.8 %shard_map.106 = bf16[8,256,640]{2,1,0:T(8,128)(2,1)} custom-call(s32[8]{0:T(128)S(1)} %select_reduce_fusion.picks, s32[4]{0:T(128)S(1)} %pad_add_fusion.sizes, bf16[7168,640]{1,0:T(8,128)(2,1)} %bitcast.14, bf16[1024,640]{1,0:T(8,128)(2,1)S(1)} %get-tuple-element.7.fresh_ref), custom_call_target="tpu_custom_call" | custom-call | tf_op jit(solution)/shard_map/pallas_call | solution.py:127
  18.1 4.4 %all-to-all-start = ((bf16[8,256,640]{2,1,0:T(8,128)(2,1)}), bf16[8,256,640]{2,1,0:T(8,128)(2,1)}, u32[]{:S(2)}, u32[]{:S(2)}) async-start(bf16[8,256,640]{2,1,0:T(8,128)(2,1)} %shard_map.106), calls=%async_computation | async-start | bytes 5242880 | tf_op jit(solution)/shard_map/all_to_all | solution.py:370
  22.5 69.1 %shard_map.105.value_ref = bf16[4,320,256]{2,1,0:T(8,128)(2,1)S(1)} custom-call(s32[4]{0:T(128)S(1)} %pad_add_fusion.sizes, bf16[5,64,1024]{2,1,0:T(8,128)(2,1)S(1)} %get-tuple-element.6.q_ref, bf16[7168,640]{1,0:T(8,128)(2,1)} %bitcast.15, bf16[1024,640]{1,0:T(8,128)(2,1)S(1)} %get-tuple-element.7.fresh_ref), custom_call_target="tpu_custom_call" | custom-call | flops 21474836480 | bytes 10485760 | tf_op jit(solution)/shard_map/pallas_call | solution.py:277
  91.6 0.0 copy-start
  91.6 0.8 copy-done
  92.4 0.0 all-to-all-done
  92.4 80.5 %shard_map.107 = (bf16[4,320,256]{2,1,0:T(8,128)(2,1)}, bf16[1,8,256,640]{3,2,1,0:T(8,128)(2,1)}) custom-call(bf16[4,320,256]{2,1,0:T(8,128)(2,1)} %copy-done, bf16[1,8,256,640]{3,2,1,0:T(8,128)(2,1)} %bitcast.7.other_ref), custom_call_target="tpu_custom_call", output_to_operand_aliasing={{0}: (0, {})} | custom-call | tf_op jit(solution)/shard_map/pallas_call | solution.py:313
  173.0 5.2 %all-to-all-start.1 = ((bf16[4,320,256]{2,1,0:T(8,128)(2,1)}), bf16[4,320,256]{2,1,0:T(8,128)(2,1)S(1)}, u32[]{:S(2)}, u32[]{:S(2)}) async-start(bf16[4,320,256]{2,1,0:T(8,128)(2,1)} %get-tuple-element.8), calls=%async_computation.1 | async-start | bytes 1310720 | tf_op jit(solution)/shard_map/all_to_all | solution.py:374
  178.2 10.5 %all-to-all-done.1 = bf16[4,320,256]{2,1,0:T(8,128)(2,1)S(1)} async-done(((bf16[4,320,256]{2,1,0:T(8,128)(2,1)}), bf16[4,320,256]{2,1,0:T(8,128)(2,1)S(1)}, u32[]{:S(2)}, u32[]{:S(2)}) %all-to-all-start.1) | async-done | bytes 655392 | tf_op jit(solution)/shard_map/all_to_all | solution.py:374
  188.7 5.3 %fusion.1 = bf16[256,2048]{1,0:T(8,128)(2,1)} fusion(bf16[1280,256]{1,0:T(8,128)(2,1)S(1)} %bitcast.16, bf16[1280,2048]{1,0:T(8,128)(2,1)} %param.13, bf16[1024,2048]{1,0:T(8,128)(2,1)} %hidden_ref.1, s32[]{:T(128)S(6)} %select_n.16, pred[256]{0:T(512)(128)(4,1)S(1)} %add_compare_fusion), kind=kOutput, calls=%fused_computation.2 | convolution fusion | flops 1344274432 | bytes 7995652 | tf_op jit(solution)/shard_map/dot_general | solution.py:375
  (4 shorter events, 0.0 us)
Async XLA Ops:
  4.1 1.3 copy-start.1
  18.1 74.4 %all-to-all-start = ((bf16[8,256,640]{2,1,0:T(8,128)(2,1)}), bf16[8,256,640]{2,1,0:T(8,128)(2,1)}, u32[]{:S(2)}, u32[]{:S(2)}) async-start(bf16[8,256,640]{2,1,0:T(8,128)(2,1)} %shard_map.106), calls=%async_computation | async-start | bytes 5242880 | tf_op jit(solution)/shard_map/all_to_all | solution.py:370
  91.6 0.8 copy-start
  173.0 15.8 %all-to-all-start.1 = ((bf16[4,320,256]{2,1,0:T(8,128)(2,1)}), bf16[4,320,256]{2,1,0:T(8,128)(2,1)S(1)}, u32[]{:S(2)}, u32[]{:S(2)}) async-start(bf16[4,320,256]{2,1,0:T(8,128)(2,1)} %get-tuple-element.8), calls=%async_computation.1 | async-start | bytes 1310720 | tf_op jit(solution)/shard_map/all_to_all | solution.py:374
